TPU v7x, 128 devices: a whole 4x4x4 slice. The times are simulated.
128 devices in a mesh: grid: 16 (over z, x), band: 8 (over y, core).
Axes of the slice: x: 4, y: 4, z: 4, core: 2. Of those that a mesh axis runs over, the one named last changes fastest.
Arguments:
- orbitals: bfloat16 [16384, 12288], P('grid', 'band'), may hold values from -1.1953125 to 1.1953125
- point_owner: int32 [4096, 1], replicated, may hold values from 0 to 15; in each aligned block of 256 rows (0 to 255, 256 to 511, ...) at most 32 rows name the same one
- point_row: int32 [4096], replicated, may hold values from 0 to 1023
- density_tiles: bfloat16 [24, 6, 512, 512], P('band'), as said below
- tile_columns: int32 [24, 6], P('band'), may hold values from 0 to 23, as said below
- tile_counts: int32 [24], P('band'), may hold values from 1 to 6, as said below
Outputs:
- exchange_rows: bfloat16 [4096, 12288], P('grid', 'band')
Inputs may be any that keep to these rules, and one draw needn't show every extreme that they name: `point_owner`: among the 256 points of each aligned block, no grid index is named more than 32 times, and some grid index is named exactly 32 times in every block. `tile_columns`: row r lists r first and then distinct tile columns; the first tile_counts[r] entries are the stored nonzero tiles. The pattern is symmetric: column c is in use in row r exactly when r is in use in row c. `tile_counts`: some tile row uses all 6 slots in every draw. `density_tiles`: the density matrix is symmetric: the tile stored in row r for column c is the transpose of the tile stored in row c for column r.
All inputs are finite; a program needn't handle non-finite values.
Results may differ from a plain program's by a relative error of at most 0.0056.
Values may be sent and summed in bfloat16 or wider, within the bound.
A program may use at most 128 MiB of HBM per device.

v0:
```python
import jax
import jax.numpy as jnp
from jax import lax
from jax.sharding import PartitionSpec as P


def screening(first, second):
    fx = (first % 16).astype(jnp.float32)
    fy = (first // 16 % 16).astype(jnp.float32)
    fz = (first // 256).astype(jnp.float32)
    sx = (second % 16).astype(jnp.float32)
    sy = (second // 16 % 16).astype(jnp.float32)
    sz = (second // 256).astype(jnp.float32)
    dist = (
        (fx[:, None] - sx[None, :]) ** 2
        + (fy[:, None] - sy[None, :]) ** 2
        + (fz[:, None] - sz[None, :]) ** 2
    )
    return 1.0 / jnp.sqrt(dist + 1.0)


def local(orbitals, point_owner, point_row, density_tiles, tile_columns, tile_counts):
    grid_count = lax.axis_size("grid")
    band_count = lax.axis_size("band")
    grid_index = lax.axis_index("grid")
    grid_rows = orbitals.shape[0]
    total_points = point_owner.shape[0]
    block_points = total_points // grid_count
    capacity = 2 * block_points // grid_count
    owners = point_owner[:, 0].reshape(grid_count, block_points)
    local_rows = point_row.reshape(grid_count, block_points)
    holder = (owners == grid_index).astype(jnp.int32)
    ahead = jnp.cumsum(holder, axis=1) - holder
    slot_ids = jnp.arange(capacity, dtype=jnp.int32)
    picked = (holder[:, :, None] == 1) & (ahead[:, :, None] == slot_ids[None, None, :])
    send_index = jnp.sum(jnp.where(picked, local_rows[:, :, None], 0), axis=1)
    outgoing = jnp.take(orbitals, send_index, axis=0)
    incoming = lax.all_to_all(outgoing, "grid", split_axis=0, concat_axis=0, tiled=True)
    own_owner = lax.dynamic_slice_in_dim(owners, grid_index, 1, 0)[0]
    point_ids = jnp.arange(block_points, dtype=jnp.int32)
    earlier = (own_owner[:, None] == own_owner[None, :]) & (point_ids[None, :] < point_ids[:, None])
    rank = jnp.sum(earlier.astype(jnp.int32), axis=1)
    flat_slot = own_owner * capacity + rank
    points = jnp.take(incoming.reshape(grid_count * capacity, -1), flat_slot, axis=0)
    tile = density_tiles.shape[-1]
    rows_local = density_tiles.shape[0]
    slots = density_tiles.shape[1]
    tile_total = rows_local * band_count
    valid = jnp.arange(slots)[None, :] < tile_counts[:, None]
    every = lax.all_gather(points, "band", axis=1, tiled=True)
    blocks = every.reshape(block_points, tile_total, tile)
    chosen = jnp.take(blocks, tile_columns, axis=1) * valid.astype(jnp.bfloat16)[None, :, :, None]
    y_float = jnp.einsum(
        "skab,pskb->sap", density_tiles, chosen, preferred_element_type=jnp.float32
    )
    y_float = y_float.reshape(rows_local * tile, block_points)
    y_t = y_float.astype(jnp.bfloat16)
    all_points = lax.all_gather(points, "grid", axis=0, tiled=True)
    all_index = point_owner[:, 0] * grid_rows + point_row
    own_index = lax.dynamic_slice_in_dim(all_index, grid_index * block_points, block_points, 0)
    pair_part = jnp.dot(all_points, y_t, preferred_element_type=jnp.float32)
    pair_t = lax.psum(pair_part, "band")
    screened = (pair_t * screening(all_index, own_index)).astype(jnp.bfloat16)
    result = lax.dot_general(
        screened, all_points, (((0,), (0,)), ((), ())), preferred_element_type=jnp.float32
    )
    return result.astype(jnp.bfloat16)


def solution(mesh):
    in_specs = (
        P("grid", "band"),
        P(),
        P(),
        P("band", None, None, None),
        P("band", None),
        P("band"),
    )
    out_specs = P("grid", "band")
    return jax.shard_map(local, mesh=mesh, in_specs=in_specs, out_specs=out_specs, check_vma=False)
```

profile of v0, /device:TPU:1, one launch (start us, length us, event | category | flops | bytes accessed | tf_op | source)
XLA Modules:
  0.0 285.2 jit_solution(6232410010118420326)
XLA Ops:
  6.5 0.0 copy-start
  6.5 0.5 broadcast.215
  7.0 1.7 broadcast_multiply_fusion
  8.7 0.7 compare_convert_fusion
  9.5 0.6 reduce-window.6
  10.1 0.2 slice_reduce_fusion
  10.3 0.7 broadcast_in_dim.61
  11.0 0.1 convert_subtract_fusion
  11.1 0.4 select_reduce_fusion
  11.5 0.1 reshape.139
  11.6 0.0 copy-done
  11.6 2.9 %gather_fusion = bf16[512,1536]{1,0:T(8,128)(2,1)} fusion(bf16[1024,1536]{1,0:T(8,128)(2,1)S(1)} %copy-done, s32[1024]{0:T(1024)S(1)} %pad_clamp_fusion.2), kind=kCustom, calls=%fused_computation | custom fusion | bytes 3147776 | tf_op jit(solution)/shard_map/jit(_take)/gather | solution.py:37
  14.5 2.8 broadcast_select_fusion
  17.3 8.5 %all-to-all-start = ((bf16[16,32,1536]{2,1,0:T(8,128)(2,1)}), bf16[16,32,1536]{2,1,0:T(8,128)(2,1)}, u32[]{:S(2)}, u32[]{:S(2)}) async-start(bf16[16,32,1536]{2,1,0:T(8,128)(2,1)} %broadcast_select_fusion), calls=%async_computation | async-start | bytes 3145728 | tf_op jit(solution)/shard_map/all_to_all | solution.py:38
  25.8 0.0 all-gather.5.cloned.1.call-start
  25.9 0.2 convert_reduce_fusion
  26.1 22.6 %all-to-all-done = bf16[16,32,1536]{2,1,0:T(8,128)(2,1)} async-done(((bf16[16,32,1536]{2,1,0:T(8,128)(2,1)}), bf16[16,32,1536]{2,1,0:T(8,128)(2,1)}, u32[]{:S(2)}, u32[]{:S(2)}) %all-to-all-start) | async-done | bytes 1572896 | tf_op jit(solution)/shard_map/all_to_all | solution.py:38
  48.7 0.0 copy-start.2
  48.7 0.0 copy-start.3
  48.7 4.5 %gather_fusion.1 = bf16[256,1536]{1,0:T(8,128)(2,1)} fusion(bf16[512,1536]{1,0:T(8,128)(2,1)} %bitcast.4, s32[1024]{0:T(1024)S(1)} %pad_clamp_fusion.1), kind=kCustom, calls=%fused_computation.1 | custom fusion | bytes 1573888 | tf_op jit(solution)/shard_map/jit(_take)/gather | solution.py:44
  53.2 2.2 broadcast_select_fusion.1
  55.4 0.0 all-gather.5.cloned.1.call-update
  55.4 0.0 all-gather.3.cloned.1.call-start
  55.5 0.7 all-gather.3.cloned.1.call-update
  56.2 0.2 all-reduce.2.cloned.1.call-start
  56.4 0.0 copy-done.2
  56.4 0.1 reshape.155
  56.5 0.0 copy-done.3
  56.5 0.1 fusion.28
  56.6 39.5 %all-gather.5.cloned.1.call-done = bf16[256,12288]{1,0:T(8,128)(2,1)} async-done(((bf16[256,1536]{1,0:T(8,128)(2,1)}), bf16[256,12288]{1,0:T(8,128)(2,1)}) %all-gather.5.cloned.1.call-update) | async-done | bytes 6291472 | tf_op jit(solution)/shard_map/all_gather | solution.py:50
  96.1 6.2 %copy.22 = bf16[32,24,8,512]{3,2,0,1:T(8,128)(2,1)} copy(bf16[32,24,8,512]{3,2,1,0:T(8,128)(2,1)} %bitcast.47) | data formatting | bytes 12582912 | tf_op jit(solution)/shard_map/reshape | solution.py:51
  102.3 6.7 %gather_fusion.2 = bf16[18,256,512]{2,1,0:T(8,128)(2,1)} fusion(bf16[256,24,512]{2,0,1:T(8,128)(2,1)} %bitcast.45, s32[1024]{0:T(1024)S(1)} %pad_clamp_fusion), kind=kCustom, calls=%fused_computation.2 | custom fusion | bytes 9437256 | tf_op jit(solution)/shard_map/jit(_take)/gather | solution.py:52
  109.0 8.9 %fusion.16 = bf16[3,512,256]{1,2,0:T(8,128)(2,1)} fusion(bf16[3,6,512,512]{3,2,1,0:T(8,128)(2,1)} %param.9, bf16[3,6,256,512]{3,2,1,0:T(8,128)(2,1)} %bitcast.46, pred[3,6]{1,0:T(4,128)(4,1)S(1)} %get-tuple-element.17, bf16[3,6]{1,0:T(4,128)(2,1)S(1)} %get-tuple-element.16), kind=kOutput, calls=%fused_computation.22 | convolution fusion | flops 2421030912 | bytes 14942262 | tf_op jit(solution)/shard_map/skab,pskb->sap/dot_general | solution.py:53
  117.8 2.4 copy.16
  120.2 67.9 %all-gather.3.cloned.1.call-done = bf16[4096,1536]{1,0:T(8,128)(2,1)} async-done(((bf16[256,1536]{1,0:T(8,128)(2,1)}), bf16[4096,1536]{1,0:T(8,128)(2,1)}) %all-gather.3.cloned.1.call-update) | async-done | bytes 12582928 | tf_op jit(solution)/shard_map/all_gather | solution.py:58
  188.0 10.1 %fusion.35 = f32[4096,256]{1,0:T(8,128)} fusion(bf16[4096,1536]{1,0:T(8,128)(2,1)} %all-gather.3.cloned.1.call-done, bf16[1536,256]{1,0:T(8,128)(2,1)} %bitcast.49), kind=kOutput, calls=%fused_computation.91 | convolution fusion | flops 3221225472 | bytes 17563648 | tf_op jit(solution)/shard_map/dot_general | solution.py:61
  198.1 0.0 copy-start.1
  198.1 0.0 all-reduce.2.cloned.1.call-update
  198.2 0.7 copy-done.1
  198.9 0.1 fusion.29
  199.0 69.7 %all-reduce.2.cloned.1.call-done = f32[4096,256]{1,0:T(8,128)} async-done(((f32[4096,256]{1,0:T(8,128)}), f32[4096,256]{1,0:T(8,128)}) %all-reduce.2.cloned.1.call-update) | async-done | bytes 4194320 | tf_op jit(solution)/shard_map/psum | solution.py:62
  268.7 10.0 %convolution_convert_fusion = bf16[256,1536]{1,0:T(8,128)(2,1)} fusion(bf16[4096,1536]{1,0:T(8,128)(2,1)} %all-gather.3.cloned.1.call-done, f32[4096,256]{1,0:T(8,128)} %all-reduce.2.cloned.1.call-done, f32[256]{0:T(256)S(1)} %get-tuple-element.11, f32[4096]{0:T(1024)S(1)} %get-tuple-element.13, f32[256]{0:T(256)S(1)} %get-tuple-element.10, ...), kind=kOutput, calls=%fused_computation.10 | convolution fusion | flops 3233153024 | bytes 17615872 | tf_op jit(solution)/shard_map/dot_general | solution.py:64
  (16 shorter events, 0.2 us)
Async XLA Ops:
  6.5 5.1 %copy-start = (bf16[1024,1536]{1,0:T(8,128)(2,1)S(1)}, bf16[1024,1536]{1,0:T(8,128)(2,1)}, u32[]{:S(2)}) copy-start(bf16[1024,1536]{1,0:T(8,128)(2,1)} %param.6) | copy-start | bytes 9437188
  17.3 31.4 %all-to-all-start = ((bf16[16,32,1536]{2,1,0:T(8,128)(2,1)}), bf16[16,32,1536]{2,1,0:T(8,128)(2,1)}, u32[]{:S(2)}, u32[]{:S(2)}) async-start(bf16[16,32,1536]{2,1,0:T(8,128)(2,1)} %broadcast_select_fusion), calls=%async_computation | async-start | bytes 3145728 | tf_op jit(solution)/shard_map/all_to_all | solution.py:38
  25.8 70.3 %all-gather.5.cloned.1.call-start = ((), (), s32[]{:S(2)}) async-start(), calls=%async_computation.2 | async-start | bytes 7077888 | tf_op jit(solution)/shard_map/all_gather | solution.py:50
  48.7 7.7 %copy-start.2 = (s32[3,6]{1,0:T(4,128)S(1)}, s32[3,6]{1,0:T(4,128)}, u32[]{:S(2)}) copy-start(s32[3,6]{1,0:T(4,128)} %param.10) | copy-start | bytes 220
  48.7 7.8 %copy-start.3 = (s32[3]{0:T(128)S(1)}, s32[3]{0:T(128)}, u32[]{:S(2)}) copy-start(s32[3]{0:T(128)} %param.11) | copy-start | bytes 40
  55.4 132.6 %all-gather.3.cloned.1.call-start = ((), (), s32[]{:S(2)}) async-start(), calls=%async_computation.1 | async-start | bytes 13369344 | tf_op jit(solution)/shard_map/all_gather | solution.py:58
  56.2 212.5 %all-reduce.2.cloned.1.call-start = ((), (), s32[]{:S(2)}) async-start(), calls=%async_computation.3 | async-start | bytes 8388608 | tf_op jit(solution)/shard_map/psum | solution.py:62
  198.1 0.7 copy-start.1
Sparse Core Ops, SparseCore 0:
  55.5 40.5 all-gather.4
  98.2 89.7 all-gather.2
  198.3 70.3 all-reduce.1
where the time goes:
time: 287 us; the launch traced here: 285 us
  waiting for transfers between devices  200 us (70%)
  matrix products  29 us (10%)
  local copies, waits for them, and re-layouts  25 us (9%)
  between operations  13.2 us (5%)
  other arithmetic  8.84 us (3%)
  starting transfers between devices  8.77 us (3%)
    psum x1, waiting for transfers between devices, local(): pair_t = lax.psum(pair_part, 'band')  69.7 us
    all_gather x1, waiting for transfers between devices, local(): all_points = lax.all_gather(points, 'grid', axis=0, tiled=True)  67.9 us
    all_gather x1, waiting for transfers between devices, local(): every = lax.all_gather(points, 'band', axis=1, tiled=True)  39.5 us
    all_to_all x1, waiting for transfers between devices, local(): lax.all_to_all(outgoing, 'grid', split_axis=0, concat_axis=0, tiled=True)  22.6 us
    dot_general x1, matrix products, local(): pair_part = jnp.dot(all_points, y_t, preferred_element_type=jnp.float32)  10.1 us
    dot_general x1, matrix products, local(): lax.dot_general(screened, all_points, (((0,), (0,)), ((), ())), preferred...  10 us
    dot_general x1, matrix products, local(): jnp.einsum('skab,pskb->sap', density_tiles, chosen, preferred_element_typ...  8.86 us
    all_to_all x1, starting transfers between devices, local(): lax.all_to_all(outgoing, 'grid', split_axis=0, concat_axis=0, tiled=True)  8.47 us
  transfers between devices with their start and end apart: 4, of which 4 were waited for; matrix products, arithmetic and copies ran while one was open for 9% of the time, Pallas kernels for 0%

commit v1 on v0

v1 whole, which is shorter than its diff:
```python
import functools

import jax
import jax.numpy as jnp
from jax import lax
from jax.experimental import pallas as pl
from jax.experimental.pallas import tpu as pltpu
from jax.sharding import PartitionSpec as P

MESH = pl.DeviceIdType.MESH
F32 = jnp.float32
BF16 = jnp.bfloat16
NCH = 4
BLK = 256
COLS = 1536
TILE = 512
CAP = 32
NSEM = 160


def nt(a, b):
    return lax.dot_general(a, b, (((1,), (1,)), ((), ())), preferred_element_type=F32)


def nn(a, b):
    return lax.dot_general(a, b, (((1,), (0,)), ((), ())), preferred_element_type=F32)


def kernel(
    owner_ref, row_ref, cols_ref, counts_ref, orb_hbm, tiles_hbm, out_ref,
    orb, tiles, onehot, slots_out, slots_in, xn, ev0, ev1, ev2, ev3, yg,
    pch, crecv, ysend, yrecv, sfull, rpart, fsend, frecv, ffwd, fsum, pos,
    ss, rs, ls,
):
    every = (ev0, ev1, ev2, ev3)
    rows = BLK // NCH
    half = rows // 2
    g = lax.axis_index("grid")
    b = lax.axis_index("band")
    z, x, y, c = g // 4, g % 4, b // 2, b % 2
    o = 1 - c

    def grid_of(zz, xx):
        return (((zz + 4) % 4) * 4 + (xx + 4) % 4, b)

    def y_of(yy):
        return (g, ((yy + 4) % 4) * 2 + c)

    core_peer = (g, y * 2 + o)
    up = lambda v, d: (v + d + 4) % 4

    counter = [0]
    open_sends = []

    def remote(src, dst, to):
        k = counter[0]
        counter[0] += 1
        return pltpu.make_async_remote_copy(
            src_ref=src, dst_ref=dst, send_sem=ss.at[k], recv_sem=rs.at[k],
            device_id=to, device_id_type=MESH,
        )

    def send(src, dst, to):
        copy = remote(src, dst, to)
        copy.start()
        open_sends.append(copy)
        return copy

    bar = pltpu.get_barrier_semaphore()
    offsets = [(dz, dx) for dz in (2, 1, 3, 0) for dx in (2, 1, 3, 0) if (dz, dx) != (0, 0)]
    for dz, dx in offsets:
        pl.semaphore_signal(bar, inc=1, device_id=grid_of(z + dz, x + dx), device_id_type=MESH)
    for dy in (1, 2, 3):
        pl.semaphore_signal(bar, inc=1, device_id=y_of(y + dy), device_id_type=MESH)
    pl.semaphore_signal(bar, inc=1, device_id=core_peer, device_id_type=MESH)

    load_orb = pltpu.make_async_copy(orb_hbm, orb, ls.at[0])
    load_orb.start()
    load_tiles = pltpu.make_async_copy(tiles_hbm, tiles, ls.at[1])
    load_tiles.start()

    owner = owner_ref[...]
    rowid = row_ref[...]
    holder = (owner == g).astype(F32)
    p0 = lax.broadcasted_iota(jnp.int32, (BLK, BLK), 0)
    p1 = lax.broadcasted_iota(jnp.int32, (BLK, BLK), 1)
    before = (p0 < p1).astype(BF16)
    ahead = nn(holder.astype(BF16), before)
    rowf = rowid.astype(F32)
    slot_id = lax.broadcasted_iota(jnp.int32, (CAP, BLK), 0).astype(F32)
    grid_row = lax.broadcasted_iota(jnp.int32, (CAP, 1024), 1).astype(F32)
    for i in range(16):
        picked = (ahead[i:i + 1, :] == slot_id) & (holder[i:i + 1, :] > 0.5)
        index = jnp.sum(jnp.where(picked, rowf[i:i + 1, :], 0.0), axis=1, keepdims=True)
        onehot[i * CAP:(i + 1) * CAP, :] = (grid_row == index).astype(F32).astype(BF16)

    index = owner * 1024 + rowid
    pos[0] = (index % 16).astype(F32)
    pos[1] = (index // 16 % 16).astype(F32)
    pos[2] = (index // 256).astype(F32)

    load_orb.wait()
    for q in range(4):
        part = slice(q * 128, (q + 1) * 128)
        slots_out[part, :] = nn(onehot[part, :], orb[...]).astype(BF16)

    pl.semaphore_wait(bar, 19)

    a_copies = []
    mine = pl.ds(pl.multiple_of(g * CAP, CAP), CAP)
    for dz, dx in offsets:
        to = grid_of(z + dz, x + dx)
        src = pl.ds(pl.multiple_of(to[0] * CAP, CAP), CAP)
        a_copies.append(send(slots_out.at[src], slots_in.at[mine], to))
    slots_in[mine, :] = slots_out[mine, :]

    own_row = owner_ref[pl.ds(g, 1), :].astype(F32)
    own_col = jnp.sum(jnp.where(p0 == p1, own_row, 0.0), axis=1, keepdims=True)
    rank = jnp.sum(
        jnp.where((own_row == own_col) & (p1 < p0), 1.0, 0.0), axis=1, keepdims=True
    )
    flat = own_col * CAP + rank
    slot_no = lax.broadcasted_iota(jnp.int32, (BLK, 16 * CAP), 1).astype(F32)
    unpermute = (slot_no == flat).astype(F32).astype(BF16)
    for copy in a_copies:
        copy.wait_recv()
    points = nn(unpermute, slots_in[...]).astype(BF16)
    xn[x] = points
    for k in range(NCH):
        for t in range(3):
            every[k][b * 3 + t] = points[k * rows:(k + 1) * rows, t * TILE:(t + 1) * TILE]

    up1, dn1, far = up(y, 1), up(y, -1), up(y, 2)
    st = {}

    def tri(yy, cc):
        return pl.ds((yy * 2 + cc) * 3, 3)

    def b_send(k):
        src = every[k].at[tri(y, c)]
        st["bp", k] = send(src, src, y_of(y + 1))
        st["bm", k] = send(src, src, y_of(y - 1))
        st["bc", k] = [send(src, src, core_peer)]

    def b_fwd(k):
        h0, h1 = pl.ds(0, half), pl.ds(half, half)
        st["bp", k].wait_recv()
        src = every[k].at[tri(dn1, c), h0]
        st["bfp", k] = send(src, src, y_of(y + 1))
        src = every[k].at[tri(dn1, c)]
        st["bc", k].append(send(src, src, core_peer))
        st["bm", k].wait_recv()
        src = every[k].at[tri(up1, c), h1]
        st["bfm", k] = send(src, src, y_of(y - 1))
        src = every[k].at[tri(up1, c)]
        st["bc", k].append(send(src, src, core_peer))

    def b_fin(k):
        st["bfp", k].wait_recv()
        st["bfm", k].wait_recv()
        src = every[k].at[tri(far, c)]
        st["bc", k].append(send(src, src, core_peer))

    def y_stage(k):
        for copy in st["bc", k]:
            copy.wait_recv()
        if k == 0:
            load_tiles.wait()
        for r in range(3):
            acc = jnp.zeros((rows, TILE), F32)
            count = counts_ref[r]
            for s in range(6):
                block = every[k][cols_ref[r, s]]
                if s > 0:
                    keep = (count > s).astype(F32)
                    block = block * keep.astype(BF16)
                acc = acc + nt(block, tiles[r * 6 + s])
            yg[z, k * rows:(k + 1) * rows, r * TILE:(r + 1) * TILE] = acc.astype(BF16)

    def c_send():
        src = xn.at[x]
        st["cp"] = send(src, src, grid_of(z, x + 1))
        st["cm"] = send(src, src, grid_of(z, x - 1))

    def c_fwd():
        st["cp"].wait_recv()
        src = xn.at[up(x, -1), pl.ds(0, 128)]
        st["cfp"] = send(src, src, grid_of(z, x + 1))
        st["cm"].wait_recv()
        src = xn.at[up(x, 1), pl.ds(128, 128)]
        st["cfm"] = send(src, src, grid_of(z, x - 1))

    def c_fin():
        st["cfp"].wait_recv()
        st["cfm"].wait_recv()

    def d_send(k):
        src = yg.at[z, pl.ds(k * rows, rows)]
        st["dp", k] = send(src, src, grid_of(z + 1, x))
        st["dm", k] = send(src, src, grid_of(z - 1, x))

    def d_fwd(k):
        st["dp", k].wait_recv()
        src = yg.at[up(z, -1), pl.ds(k * rows, half)]
        st["dfp", k] = send(src, src, grid_of(z + 1, x))
        st["dm", k].wait_recv()
        src = yg.at[up(z, 1), pl.ds(k * rows + half, half)]
        st["dfm", k] = send(src, src, grid_of(z - 1, x))

    def pair(k):
        st["dfp", k].wait_recv()
        st["dfm", k].wait_recv()
        lhs = yg[:, k * rows:(k + 1) * rows, :].reshape(4 * rows, COLS)
        for h in range(2):
            rhs = xn[2 * h:2 * h + 2].reshape(2 * BLK, COLS)
            pch[k, h] = nt(lhs, rhs)
        st["e1", k] = send(pch.at[k, o], crecv.at[k], core_peer)

    def e2(k):
        st["e1", k].wait_recv()
        total = pch[k, c] + crecv[k]
        pch[k, c] = total
        ysend[k] = total.astype(BF16).reshape(4, rows, TILE)
        for d in (2, 1, 3):
            st["e2", k, d] = send(
                ysend.at[k, up(y, d)], yrecv.at[k, d - 1], y_of(y + d)
            )

    def e3(k):
        mine = pl.ds(pl.multiple_of(y * rows, rows), rows)
        total = pch[k, c, mine, :]
        for d in (1, 2, 3):
            st["e2", k, d].wait_recv()
            total = total + yrecv[k, d - 1].astype(F32)
        eye0 = lax.broadcasted_iota(jnp.int32, (rows, BLK), 0) + k * rows
        eye1 = lax.broadcasted_iota(jnp.int32, (rows, BLK), 1)
        eye = eye0 == eye1
        sides = []
        mu_at = [
            jnp.sum(jnp.where(eye, pos[a, pl.ds(y * 4 + x, 1), :], 0.0), axis=1, keepdims=True)
            for a in range(3)
        ]
        for h in range(2):
            dist = jnp.ones((rows, BLK), F32)
            for a in range(3):
                delta = mu_at[a] - pos[a, pl.ds(z * 4 + 2 * c + h, 1), :]
                dist = dist + delta * delta
            sides.append(lax.rsqrt(dist))
        kern = jnp.concatenate(sides, axis=1)
        sfull[k, c, y] = (total * kern).astype(BF16)
        src = sfull.at[k, c, y]
        for d in (2, 1, 3):
            st["e3", k, d] = send(src, src, y_of(y + d))

    def e4(k):
        for d in (1, 2, 3):
            st["e3", k, d].wait_recv()
        src = sfull.at[k, c]
        st["e4", k] = send(src, src, core_peer)

    def res(k):
        st["e4", k].wait_recv()
        total = nn(sfull[k, 0].reshape(4 * rows, 2 * BLK), xn[0:2].reshape(2 * BLK, COLS))
        total = total + nn(sfull[k, 1].reshape(4 * rows, 2 * BLK), xn[2:4].reshape(2 * BLK, COLS))
        rpart[k] = total.reshape(4, rows, COLS)
        fsend[k] = total.astype(BF16).reshape(4, rows, COLS)
        far_z, up_z, dn_z = up(z, 2), up(z, 1), up(z, -1)
        lo, hi = pl.ds(0, half), pl.ds(half, half)
        st["fp", k] = send(fsend.at[k, far_z, lo], ffwd.at[k, 0], grid_of(z + 1, x))
        st["fm", k] = send(fsend.at[k, far_z, hi], ffwd.at[k, 1], grid_of(z - 1, x))
        st["fdp", k] = send(fsend.at[k, up_z, hi], frecv.at[k, 0], grid_of(z + 1, x))
        st["fdm", k] = send(fsend.at[k, dn_z, lo], frecv.at[k, 1], grid_of(z - 1, x))

    def f_fwd(k):
        up_z, dn_z = up(z, 1), up(z, -1)
        st["fp", k].wait_recv()
        fsum[k, 0] = (rpart[k, up_z, 0:half, :] + ffwd[k, 0].astype(F32)).astype(BF16)
        st["fsp", k] = send(fsum.at[k, 0], frecv.at[k, 2], grid_of(z + 1, x))
        st["fm", k].wait_recv()
        fsum[k, 1] = (rpart[k, dn_z, half:rows, :] + ffwd[k, 1].astype(F32)).astype(BF16)
        st["fsm", k] = send(fsum.at[k, 1], frecv.at[k, 3], grid_of(z - 1, x))

    def f_fin(k):
        for name in ("fdp", "fdm", "fsp", "fsm"):
            st[name, k].wait_recv()
        lo = rpart[k, z, 0:half, :] + frecv[k, 2].astype(F32) + frecv[k, 1].astype(F32)
        hi = rpart[k, z, half:rows, :] + frecv[k, 0].astype(F32) + frecv[k, 3].astype(F32)
        out_ref[k * rows:k * rows + half, :] = lo.astype(BF16)
        out_ref[k * rows + half:(k + 1) * rows, :] = hi.astype(BF16)

    b_send(0)
    c_send()
    for t in range(1, NCH + 8):
        def at(offset):
            k = t - offset
            return k if 0 <= k < NCH else None

        if t < NCH:
            b_send(t)
        if at(1) is not None:
            b_fwd(t - 1)
            b_fin(t - 1)
            y_stage(t - 1)
            d_send(t - 1)
        if t == 2:
            c_fwd()
        if at(2) is not None:
            d_fwd(t - 2)
        if t == 3:
            c_fin()
        if at(5) is not None:
            e3(t - 5)
        if at(6) is not None:
            e4(t - 6)
        if at(4) is not None:
            e2(t - 4)
        if at(3) is not None:
            pair(t - 3)
        if at(6) is not None:
            res(t - 6)
        if at(7) is not None:
            f_fwd(t - 7)
    for k in range(NCH):
        f_fin(k)
    for copy in open_sends:
        copy.wait_send()


def local(orbitals, point_owner, point_row, density_tiles, tile_columns, tile_counts):
    rows = BLK // NCH
    half = rows // 2
    vmem = pl.BlockSpec(memory_space=pltpu.VMEM)
    smem = pl.BlockSpec(memory_space=pltpu.SMEM)
    hbm = pl.BlockSpec(memory_space=pl.ANY)
    return pl.pallas_call(
        kernel,
        name="exchange",
        out_shape=jax.ShapeDtypeStruct((BLK, COLS), BF16),
        in_specs=[vmem, vmem, smem, smem, hbm, hbm],
        out_specs=vmem,
        scratch_shapes=[
            pltpu.VMEM((1024, COLS), BF16),
            pltpu.VMEM((18, TILE, TILE), BF16),
            pltpu.VMEM((512, 1024), BF16),
            pltpu.VMEM((512, COLS), BF16),
            pltpu.VMEM((512, COLS), BF16),
            pltpu.VMEM((4, BLK, COLS), BF16),
            pltpu.VMEM((24, rows, TILE), BF16),
            pltpu.VMEM((24, rows, TILE), BF16),
            pltpu.VMEM((24, rows, TILE), BF16),
            pltpu.VMEM((24, rows, TILE), BF16),
            pltpu.VMEM((4, BLK, COLS), BF16),
            pltpu.VMEM((NCH, 2, 4 * rows, TILE), F32),
            pltpu.VMEM((NCH, 4 * rows, TILE), F32),
            pltpu.VMEM((NCH, 4, rows, TILE), BF16),
            pltpu.VMEM((NCH, 3, rows, TILE), BF16),
            pltpu.VMEM((NCH, 2, 4, rows, TILE), BF16),
            pltpu.VMEM((NCH, 4, rows, COLS), F32),
            pltpu.VMEM((NCH, 4, rows, COLS), BF16),
            pltpu.VMEM((NCH, 4, half, COLS), BF16),
            pltpu.VMEM((NCH, 2, half, COLS), BF16),
            pltpu.VMEM((NCH, 2, half, COLS), BF16),
            pltpu.VMEM((3, 16, BLK), F32),
            pltpu.SemaphoreType.DMA((NSEM,)),
            pltpu.SemaphoreType.DMA((NSEM,)),
            pltpu.SemaphoreType.DMA((2,)),
        ],
        compiler_params=pltpu.CompilerParams(
            collective_id=0, has_side_effects=True, vmem_limit_bytes=60 * 2**20
        ),
        cost_estimate=pl.CostEstimate(
            flops=12_000_000_000, bytes_accessed=14_000_000, transcendentals=0
        ),
    )(
        point_owner.reshape(16, BLK),
        point_row.reshape(16, BLK),
        tile_columns,
        tile_counts,
        orbitals,
        density_tiles.reshape(18, TILE, TILE),
    )


def solution(mesh):
    in_specs = (
        P("grid", "band"),
        P(),
        P(),
        P("band", None, None, None),
        P("band", None),
        P("band"),
    )
    return jax.shard_map(
        local, mesh=mesh, in_specs=in_specs, out_specs=P("grid", "band"), check_vma=False
    )
```

time: 287 us -> 142 us (0.49)
  waiting for transfers between devices: 200 us -> 0 us
  Pallas kernels: 0 us -> 136 us
  matrix products: 29 us -> 0 us
  local copies, waits for them, and re-layouts: 25 us -> 4.51 us
  between operations: 13.2 us -> 0.01 us
  starting transfers between devices: 8.77 us -> 0 us
  other arithmetic: 8.84 us -> 1.4 us
    pallas_call x0 -> x1, Pallas kernels: none -> 136 us  [local(): pl.pallas_call(kernel, name='exchange', out_shape=jax.ShapeDtypeStruct((B...]
    all_gather x2 -> x0, waiting for transfers between devices: 107 us -> none  [the longest x1 67.9 us: local(): all_points = lax.all_gather(points, 'grid', axis=0, tiled=True)]
    psum x1 -> x0, waiting for transfers between devices: 69.7 us -> none  [local(): pair_t = lax.psum(pair_part, 'band')]
    dot_general x3 -> x0, matrix products: 29 us -> none  [the longest x1 10.1 us: local(): pair_part = jnp.dot(all_points, y_t, preferred_element_type=jnp.float32)]
    all_to_all x1 -> x0, waiting for transfers between devices: 22.6 us -> none  [local(): lax.all_to_all(outgoing, 'grid', split_axis=0, concat_axis=0, tiled=True)]
    gather x3 -> x0, local copies, waits for them, and re-layouts: 14.2 us -> none  [the longest x1 6.71 us: local(): jnp.take(blocks, tile_columns, axis=1)]
    all_to_all x1 -> x0, starting transfers between devices: 8.47 us -> none  [local(): lax.all_to_all(outgoing, 'grid', split_axis=0, concat_axis=0, tiled=True)]
    select_n x5 -> x0, other arithmetic: 4.95 us -> none  [the longest x2 2.78 us: local(): outgoing = jnp.take(orbitals, send_index, axis=0)]
  transfers between devices with their start and end apart: 4 -> 0, of which waited for: 4 -> 0; matrix products, arithmetic and copies ran while one was open for 9% -> 0% of each run, Pallas kernels for 0% -> 0%
where the time goes in v1:
time: 142 us
  Pallas kernels  136 us (96%)
  local copies, waits for them, and re-layouts  4.51 us (3%)
    pallas_call x1, Pallas kernels, local(): pl.pallas_call(kernel, name='exchange', out_shape=jax.ShapeDtypeStruct((B...  136 us

profile of v1, /device:TPU:1, one launch (start us, length us, event | category | flops | bytes accessed | tf_op | source)
XLA Modules:
  0.0 141.7 jit_solution(13711142716394871687)
XLA Ops:
  0.0 0.5 broadcast.3
  0.5 1.4 reduce.3
  1.9 0.6 reshape.9.owner_ref
  2.5 1.3 reshape.10.row_ref
  3.8 135.7 %exchange.1 = bf16[256,1536]{1,0:T(8,128)(2,1)} custom-call(s32[16,256]{1,0:T(8,128)} %reshape.9.owner_ref, s32[16,256]{1,0:T(8,128)} %reshape.10.row_ref, s32[3,6]{1,0:T(4,128)} %cols_ref.1, s32[3]{0:T(128)} %counts_ref.1, bf16[1024,1536]{1,0:T(8,128)(2,1)} %orb_hbm.1, bf16[18,512,512]{2,1,0:T(8,128)(2,1)} %bitcast.2), custom_call_target="tpu_custom_call" | custom-call | flops 12000000000 | bytes 14000000 | tf_op jit(solution)/shard_map/exchange/pallas_call | solution.py:335
  139.6 2.1 %copy.8 = bf16[256,1536]{1,0:T(8,128)(2,1)} copy(bf16[256,1536]{1,0:T(8,128)(2,1)} %exchange.1) | data formatting | bytes 1572864

commit v2 on v1

v2 whole, which is shorter than its diff:
```python
import functools

import jax
import jax.numpy as jnp
from jax import lax
from jax.experimental import pallas as pl
from jax.experimental.pallas import tpu as pltpu
from jax.sharding import PartitionSpec as P

MESH = pl.DeviceIdType.MESH
F32 = jnp.float32
BF16 = jnp.bfloat16
NCH = 4
BLK = 256
COLS = 1536
TILE = 512
CAP = 32
NSEM = 192


def nt(a, b):
    return lax.dot_general(a, b, (((1,), (1,)), ((), ())), preferred_element_type=F32)


def nn(a, b):
    return lax.dot_general(a, b, (((1,), (0,)), ((), ())), preferred_element_type=F32)


def kernel(
    index_ref, cols_ref, counts_ref, orb_hbm, tiles_hbm, out_ref,
    orb, tiles, onehot, slots_out, slots_in, xn, ev0, ev1, ev2, ev3, yg,
    pch, crecv, ysend, yrecv, sfull, rpart, fsend, frecv, ffwd, fsum, pos,
    ss, rs, ls,
):
    every = (ev0, ev1, ev2, ev3)
    rows = BLK // NCH
    half = rows // 2
    g = lax.axis_index("grid")
    b = lax.axis_index("band")
    z, x, y, c = g // 4, g % 4, b // 2, b % 2
    o = 1 - c

    def grid_of(zz, xx):
        return (((zz + 4) % 4) * 4 + (xx + 4) % 4, b)

    def y_of(yy):
        return (g, ((yy + 4) % 4) * 2 + c)

    core_peer = (g, y * 2 + o)
    up = lambda v, d: (v + d + 4) % 4

    place = (z, x)

    def ring(mode, d):
        return grid_of(z + d, x) if mode == 0 else grid_of(z, x + d)

    counter = [0]
    open_sends = []

    def send(src, dst, to):
        k = counter[0]
        counter[0] += 1
        copy = pltpu.make_async_remote_copy(
            src_ref=src, dst_ref=dst, send_sem=ss.at[k], recv_sem=rs.at[k],
            device_id=to, device_id_type=MESH,
        )
        copy.start()
        open_sends.append(copy)
        return copy

    bar = pltpu.get_barrier_semaphore()
    for dz in (2, 1, 3, 0):
        for dx in (2, 1, 3, 0):
            if (dz, dx) != (0, 0):
                pl.semaphore_signal(
                    bar, inc=1, device_id=grid_of(z + dz, x + dx), device_id_type=MESH
                )
    for dy in (1, 2, 3):
        pl.semaphore_signal(bar, inc=1, device_id=y_of(y + dy), device_id_type=MESH)
    pl.semaphore_signal(bar, inc=1, device_id=core_peer, device_id_type=MESH)

    load_orb = pltpu.make_async_copy(orb_hbm, orb, ls.at[0])
    load_orb.start()
    load_tiles = pltpu.make_async_copy(tiles_hbm, tiles, ls.at[1])
    load_tiles.start()

    index = index_ref[...]
    owner = index // 1024
    rowf = (index % 1024).astype(F32)
    holder = (owner == g).astype(F32)
    p0 = lax.broadcasted_iota(jnp.int32, (BLK, BLK), 0)
    p1 = lax.broadcasted_iota(jnp.int32, (BLK, BLK), 1)
    before = (p0 < p1).astype(BF16)
    ahead = nn(holder.astype(BF16), before)
    slot_id = lax.broadcasted_iota(jnp.int32, (CAP, BLK), 0).astype(F32)
    grid_row = lax.broadcasted_iota(jnp.int32, (CAP, 1024), 1).astype(F32)
    for i in range(16):
        picked = (ahead[i:i + 1, :] == slot_id) & (holder[i:i + 1, :] > 0.5)
        wanted = jnp.sum(jnp.where(picked, rowf[i:i + 1, :], 0.0), axis=1, keepdims=True)
        onehot[i * CAP:(i + 1) * CAP, :] = (grid_row == wanted).astype(F32).astype(BF16)

    load_orb.wait()
    a_copies = []
    mine = pl.ds(pl.multiple_of(g * CAP, CAP), CAP)
    for q in range(3):
        piece = []
        for dz in (2, 1, 3, 0):
            part = pl.ds(pl.multiple_of(up(z, dz) * 128, 128), 128)
            slots_out[q, part, :] = nn(
                onehot[part, :], orb[:, q * TILE:(q + 1) * TILE]
            ).astype(BF16)
            if q == 0 and dz == 2:
                pl.semaphore_wait(bar, 19)
            for dx in (2, 1, 3, 0):
                if (dz, dx) == (0, 0):
                    continue
                to = grid_of(z + dz, x + dx)
                src = pl.ds(pl.multiple_of(to[0] * CAP, CAP), CAP)
                piece.append(send(slots_out.at[q, src], slots_in.at[q, mine], to))
        slots_in[q, mine, :] = slots_out[q, mine, :]
        a_copies.append(piece)

    pos[0] = (index % 16).astype(F32)
    pos[1] = (index // 16 % 16).astype(F32)
    pos[2] = (index // 256).astype(F32)
    own_row = (index_ref[pl.ds(g, 1), :] // 1024).astype(F32)
    own_col = jnp.sum(jnp.where(p0 == p1, own_row, 0.0), axis=1, keepdims=True)
    rank = jnp.sum(
        jnp.where((own_row == own_col) & (p1 < p0), 1.0, 0.0), axis=1, keepdims=True
    )
    flat = own_col * CAP + rank
    slot_no = lax.broadcasted_iota(jnp.int32, (BLK, 16 * CAP), 1).astype(F32)
    unpermute = (slot_no == flat).astype(F32).astype(BF16)

    st = {}

    def a_fin(q):
        for copy in a_copies[q]:
            copy.wait_recv()
        points = nn(unpermute, slots_in[q]).astype(BF16)
        xn[0, q, x] = points
        xn[1, q, z] = points
        for k in range(NCH):
            every[k][c * 12 + q * 4 + y] = points[k * rows:(k + 1) * rows, :]

    def b_send(q, k):
        src = every[k].at[c * 12 + q * 4 + y]
        st["b", q, k] = [send(src, src, y_of(y + d)) for d in (2, 1, 3)]

    def b_core(q, k):
        for copy in st["b", q, k]:
            copy.wait_recv()
        src = every[k].at[pl.ds(c * 12 + q * 4, 4)]
        st["bc", q, k] = send(src, src, core_peer)

    def y_stage(k):
        for q in range(3):
            st["bc", q, k].wait_recv()
        if k == 0:
            load_tiles.wait()
        for r in range(3):
            acc = jnp.zeros((rows, TILE), F32)
            count = counts_ref[r]
            for s in range(6):
                col = cols_ref[r, s]
                block = every[k][(col // 3 % 2) * 12 + (col % 3) * 4 + col // 6]
                if s > 0:
                    keep = (count > s).astype(F32)
                    block = block * keep.astype(BF16)
                acc = acc + nt(block, tiles[r * 6 + s])
            yg[place_of(k), k * rows:(k + 1) * rows, r * TILE:(r + 1) * TILE] = acc.astype(BF16)

    def place_of(k):
        return place[k % 2]

    def c_send(q):
        for mode in range(2):
            v = place[1 - mode]
            src = xn.at[mode, q, v]
            st["c", q, mode] = [send(src, src, ring(1 - mode, d)) for d in (1, -1)]

    def c_fwd(q):
        for mode in range(2):
            v = place[1 - mode]
            plus, minus = st["c", q, mode]
            plus.wait_recv()
            src = xn.at[mode, q, up(v, -1), pl.ds(0, 128)]
            ahead_copy = send(src, src, ring(1 - mode, 1))
            minus.wait_recv()
            src = xn.at[mode, q, up(v, 1), pl.ds(128, 128)]
            st["cf", q, mode] = (ahead_copy, send(src, src, ring(1 - mode, -1)))

    def c_fin(q):
        for mode in range(2):
            for copy in st["cf", q, mode]:
                copy.wait_recv()

    def d_send(k):
        src = yg.at[place_of(k), pl.ds(k * rows, rows)]
        st["dp", k] = send(src, src, ring(k % 2, 1))
        st["dm", k] = send(src, src, ring(k % 2, -1))

    def d_fwd(k):
        st["dp", k].wait_recv()
        src = yg.at[up(place_of(k), -1), pl.ds(k * rows, half)]
        st["dfp", k] = send(src, src, ring(k % 2, 1))
        st["dm", k].wait_recv()
        src = yg.at[up(place_of(k), 1), pl.ds(k * rows + half, half)]
        st["dfm", k] = send(src, src, ring(k % 2, -1))

    def pair(k):
        st["dfp", k].wait_recv()
        st["dfm", k].wait_recv()
        mode = k % 2
        for h in (o, c):
            total = None
            for q in range(3):
                lhs = yg[:, k * rows:(k + 1) * rows, q * TILE:(q + 1) * TILE]
                rhs = xn[mode, q, pl.ds(2 * h, 2)]
                term = nt(lhs.reshape(4 * rows, TILE), rhs.reshape(2 * BLK, TILE))
                total = term if total is None else total + term
            pch[k, h] = total
            if h is o:
                st["e1", k] = send(pch.at[k, o], crecv.at[k], core_peer)

    def e2(k):
        st["e1", k].wait_recv()
        total = pch[k, c] + crecv[k]
        pch[k, c] = total
        ysend[k] = total.astype(BF16).reshape(4, rows, TILE)
        for d in (2, 1, 3):
            st["e2", k, d] = send(
                ysend.at[k, up(y, d)], yrecv.at[k, d - 1], y_of(y + d)
            )

    def e3(k):
        part = pl.ds(pl.multiple_of(y * rows, rows), rows)
        total = pch[k, c, part, :]
        for d in (1, 2, 3):
            st["e2", k, d].wait_recv()
            total = total + yrecv[k, d - 1].astype(F32)
        eye0 = lax.broadcasted_iota(jnp.int32, (rows, BLK), 0) + k * rows
        eye1 = lax.broadcasted_iota(jnp.int32, (rows, BLK), 1)
        eye = eye0 == eye1
        mu_block = y * 4 + x if k % 2 == 0 else z * 4 + y
        sides = []
        mu_at = [
            jnp.sum(jnp.where(eye, pos[a, pl.ds(mu_block, 1), :], 0.0), axis=1, keepdims=True)
            for a in range(3)
        ]
        for h in range(2):
            nu_block = z * 4 + 2 * c + h if k % 2 == 0 else (2 * c + h) * 4 + x
            dist = jnp.ones((rows, BLK), F32)
            for a in range(3):
                delta = mu_at[a] - pos[a, pl.ds(nu_block, 1), :]
                dist = dist + delta * delta
            sides.append(lax.rsqrt(dist))
        kern = jnp.concatenate(sides, axis=1)
        sfull[k, c, y] = (total * kern).astype(BF16)
        src = sfull.at[k, c, y]
        for d in (2, 1, 3):
            st["e3", k, d] = send(src, src, y_of(y + d))

    def e4(k):
        for d in (1, 2, 3):
            st["e3", k, d].wait_recv()
        src = sfull.at[k, c]
        st["e4", k] = send(src, src, core_peer)

    def res(k):
        st["e4", k].wait_recv()
        mode = k % 2
        lhs = [sfull[k, h].reshape(4 * rows, 2 * BLK) for h in range(2)]
        for q in range(3):
            total = nn(lhs[0], xn[mode, q, 0:2].reshape(2 * BLK, TILE))
            total = total + nn(lhs[1], xn[mode, q, 2:4].reshape(2 * BLK, TILE))
            cut = slice(q * TILE, (q + 1) * TILE)
            rpart[k, :, :, cut] = total.reshape(4, rows, TILE)
            fsend[k, :, :, cut] = total.astype(BF16).reshape(4, rows, TILE)
        v = place_of(k)
        far_v, up_v, dn_v = up(v, 2), up(v, 1), up(v, -1)
        lo, hi = pl.ds(0, half), pl.ds(half, half)
        st["fp", k] = send(fsend.at[k, far_v, lo], ffwd.at[k, 0], ring(mode, 1))
        st["fm", k] = send(fsend.at[k, far_v, hi], ffwd.at[k, 1], ring(mode, -1))
        st["fdp", k] = send(fsend.at[k, up_v, hi], frecv.at[k, 0], ring(mode, 1))
        st["fdm", k] = send(fsend.at[k, dn_v, lo], frecv.at[k, 1], ring(mode, -1))

    def f_fwd(k):
        up_v, dn_v = up(place_of(k), 1), up(place_of(k), -1)
        st["fp", k].wait_recv()
        fsum[k, 0] = (rpart[k, up_v, 0:half, :] + ffwd[k, 0].astype(F32)).astype(BF16)
        st["fsp", k] = send(fsum.at[k, 0], frecv.at[k, 2], ring(k % 2, 1))
        st["fm", k].wait_recv()
        fsum[k, 1] = (rpart[k, dn_v, half:rows, :] + ffwd[k, 1].astype(F32)).astype(BF16)
        st["fsm", k] = send(fsum.at[k, 1], frecv.at[k, 3], ring(k % 2, -1))

    def f_fin(k):
        v = place_of(k)
        for name in ("fdp", "fdm", "fsp", "fsm"):
            st[name, k].wait_recv()
        lo = rpart[k, v, 0:half, :] + frecv[k, 2].astype(F32) + frecv[k, 1].astype(F32)
        hi = rpart[k, v, half:rows, :] + frecv[k, 0].astype(F32) + frecv[k, 3].astype(F32)
        out_ref[k * rows:k * rows + half, :] = lo.astype(BF16)
        out_ref[k * rows + half:(k + 1) * rows, :] = hi.astype(BF16)

    steps = []
    for q in range(3):
        steps += [(a_fin, q)] + [(b_send, q, k) for k in range(NCH)] + [(c_send, q)]
    steps += [(b_core, 0, k) for k in range(NCH)] + [(b_core, 1, k) for k in range(NCH)]
    steps += [
        (b_core, 2, 0), (c_fwd, 0), (y_stage, 0), (d_send, 0),
        (b_core, 2, 1), (y_stage, 1), (d_send, 1),
        (c_fwd, 1), (b_core, 2, 2), (y_stage, 2), (d_send, 2),
        (b_core, 2, 3), (y_stage, 3), (d_send, 3),
        (c_fwd, 2), (d_fwd, 0), (d_fwd, 1), (c_fin, 0), (c_fin, 1), (c_fin, 2),
        (pair, 0), (pair, 1), (d_fwd, 2), (e2, 0), (e2, 1), (d_fwd, 3),
        (e3, 0), (pair, 2), (e3, 1), (pair, 3),
        (e4, 0), (e2, 2), (e4, 1), (e2, 3),
        (res, 0), (e3, 2), (res, 1), (e3, 3), (e4, 2), (e4, 3),
        (f_fwd, 0), (f_fwd, 1), (res, 2), (res, 3), (f_fwd, 2), (f_fwd, 3),
    ]
    steps += [(f_fin, k) for k in range(NCH)]
    for stage, *at in steps:
        stage(*at)
    for copy in open_sends:
        copy.wait_send()


def local(orbitals, point_owner, point_row, density_tiles, tile_columns, tile_counts):
    rows = BLK // NCH
    half = rows // 2
    vmem = pl.BlockSpec(memory_space=pltpu.VMEM)
    smem = pl.BlockSpec(memory_space=pltpu.SMEM)
    hbm = pl.BlockSpec(memory_space=pl.ANY)
    return pl.pallas_call(
        kernel,
        name="exchange",
        out_shape=jax.ShapeDtypeStruct((BLK, COLS), BF16),
        in_specs=[vmem, smem, smem, hbm, hbm],
        out_specs=vmem,
        scratch_shapes=[
            pltpu.VMEM((1024, COLS), BF16),
            pltpu.VMEM((18, TILE, TILE), BF16),
            pltpu.VMEM((512, 1024), BF16),
            pltpu.VMEM((3, 512, TILE), BF16),
            pltpu.VMEM((3, 512, TILE), BF16),
            pltpu.VMEM((2, 3, 4, BLK, TILE), BF16),
            pltpu.VMEM((24, rows, TILE), BF16),
            pltpu.VMEM((24, rows, TILE), BF16),
            pltpu.VMEM((24, rows, TILE), BF16),
            pltpu.VMEM((24, rows, TILE), BF16),
            pltpu.VMEM((4, BLK, COLS), BF16),
            pltpu.VMEM((NCH, 2, 4 * rows, TILE), F32),
            pltpu.VMEM((NCH, 4 * rows, TILE), F32),
            pltpu.VMEM((NCH, 4, rows, TILE), BF16),
            pltpu.VMEM((NCH, 3, rows, TILE), BF16),
            pltpu.VMEM((NCH, 2, 4, rows, TILE), BF16),
            pltpu.VMEM((NCH, 4, rows, COLS), F32),
            pltpu.VMEM((NCH, 4, rows, COLS), BF16),
            pltpu.VMEM((NCH, 4, half, COLS), BF16),
            pltpu.VMEM((NCH, 2, half, COLS), BF16),
            pltpu.VMEM((NCH, 2, half, COLS), BF16),
            pltpu.VMEM((3, 16, BLK), F32),
            pltpu.SemaphoreType.DMA((NSEM,)),
            pltpu.SemaphoreType.DMA((NSEM,)),
            pltpu.SemaphoreType.DMA((2,)),
        ],
        compiler_params=pltpu.CompilerParams(
            collective_id=0, has_side_effects=True, vmem_limit_bytes=60 * 2**20
        ),
        cost_estimate=pl.CostEstimate(
            flops=12_000_000_000, bytes_accessed=14_000_000, transcendentals=0
        ),
    )(
        (point_owner[:, 0] * 1024 + point_row).reshape(16, BLK),
        tile_columns,
        tile_counts,
        orbitals,
        density_tiles.reshape(18, TILE, TILE),
    )


def solution(mesh):
    in_specs = (
        P("grid", "band"),
        P(),
        P(),
        P("band", None, None, None),
        P("band", None),
        P("band"),
    )
    return jax.shard_map(
        local, mesh=mesh, in_specs=in_specs, out_specs=P("grid", "band"), check_vma=False
    )
```

time: 142 us -> 125 us (0.88)
  Pallas kernels: 136 us -> 120 us
  local copies, waits for them, and re-layouts: 4.51 us -> 2.68 us
    pallas_call x1, Pallas kernels: 136 us -> 120 us  [local(): pl.pallas_call(kernel, name='exchange', out_shape=jax.ShapeDtypeStruct((B...]
where the time goes in v2:
time: 125 us; the launch traced here: 124 us
  Pallas kernels  120 us (96%)
  local copies, waits for them, and re-layouts  2.68 us (2%)
  other arithmetic  1.46 us (1%)
    pallas_call x1, Pallas kernels, local(): pl.pallas_call(kernel, name='exchange', out_shape=jax.ShapeDtypeStruct((B...  120 us

profile of v2, /device:TPU:1, one launch (start us, length us, event | category | flops | bytes accessed | tf_op | source)
XLA Modules:
  0.0 124.1 jit_solution(7799434619208196429)
XLA Ops:
  0.0 0.7 broadcast_multiply_fusion
  0.7 0.7 add.3
  1.5 0.6 reshape.8.index_ref
  2.1 120.0 %exchange.1 = bf16[256,1536]{1,0:T(8,128)(2,1)} custom-call(s32[16,256]{1,0:T(8,128)} %reshape.8.index_ref, s32[3,6]{1,0:T(4,128)} %cols_ref.1, s32[3]{0:T(128)} %counts_ref.1, bf16[1024,1536]{1,0:T(8,128)(2,1)} %orb_hbm.1, bf16[18,512,512]{2,1,0:T(8,128)(2,1)} %bitcast.3), custom_call_target="tpu_custom_call" | custom-call | flops 12000000000 | bytes 14000000 | tf_op jit(solution)/shard_map/exchange/pallas_call | solution.py:335
  122.1 2.1 %copy.8 = bf16[256,1536]{1,0:T(8,128)(2,1)} copy(bf16[256,1536]{1,0:T(8,128)(2,1)} %exchange.1) | data formatting | bytes 1572864

commit v3 on v2

--- a/solution.py
+++ b/solution.py
@@ -16,6 +16,7 @@
 TILE = 512
 CAP = 32
 NSEM = 192
+WINDOW = 3
 
 
 def nt(a, b):
@@ -100,25 +101,40 @@
         onehot[i * CAP:(i + 1) * CAP, :] = (grid_row == wanted).astype(F32).astype(BF16)
 
     load_orb.wait()
+    mine = pl.ds(pl.multiple_of(g * CAP, CAP), CAP)
+    pieces = [(q, dz) for q in range(3) for dz in (2, 1, 3, 0)]
     a_copies = []
-    mine = pl.ds(pl.multiple_of(g * CAP, CAP), CAP)
-    for q in range(3):
-        piece = []
-        for dz in (2, 1, 3, 0):
-            part = pl.ds(pl.multiple_of(up(z, dz) * 128, 128), 128)
-            slots_out[q, part, :] = nn(
-                onehot[part, :], orb[:, q * TILE:(q + 1) * TILE]
-            ).astype(BF16)
-            if q == 0 and dz == 2:
-                pl.semaphore_wait(bar, 19)
-            for dx in (2, 1, 3, 0):
-                if (dz, dx) == (0, 0):
-                    continue
+
+    def a_rows(s):
+        q, dz = pieces[s]
+        part = pl.ds(pl.multiple_of(up(z, dz) * 128, 128), 128)
+        slots_out[q, part, :] = nn(
+            onehot[part, :], orb[:, q * TILE:(q + 1) * TILE]
+        ).astype(BF16)
+
+    def a_send(s):
+        if s >= WINDOW:
+            for copy in a_copies[s - WINDOW]:
+                copy.wait_send()
+                open_sends[:] = [other for other in open_sends if other is not copy]
+        q, dz = pieces[s]
+        group = []
+        for dx in (2, 1, 3, 0):
+            if (dz, dx) != (0, 0):
                 to = grid_of(z + dz, x + dx)
                 src = pl.ds(pl.multiple_of(to[0] * CAP, CAP), CAP)
-                piece.append(send(slots_out.at[q, src], slots_in.at[q, mine], to))
+                group.append(send(slots_out.at[q, src], slots_in.at[q, mine], to))
+        a_copies.append(group)
+
+    for s in range(WINDOW):
+        a_rows(s)
+        if s == 0:
+            pl.semaphore_wait(bar, 19)
+        a_send(s)
+    for s in range(WINDOW, 12):
+        a_rows(s)
+    for q in range(3):
         slots_in[q, mine, :] = slots_out[q, mine, :]
-        a_copies.append(piece)
 
     pos[0] = (index % 16).astype(F32)
     pos[1] = (index // 16 % 16).astype(F32)
@@ -135,8 +151,9 @@
     st = {}
 
     def a_fin(q):
-        for copy in a_copies[q]:
-            copy.wait_recv()
+        for group in a_copies[4 * q:4 * q + 4]:
+            for copy in group:
+                copy.wait_recv()
         points = nn(unpermute, slots_in[q]).astype(BF16)
         xn[0, q, x] = points
         xn[1, q, z] = points
@@ -303,16 +320,19 @@
         out_ref[k * rows:k * rows + half, :] = lo.astype(BF16)
         out_ref[k * rows + half:(k + 1) * rows, :] = hi.astype(BF16)
 
-    steps = []
-    for q in range(3):
-        steps += [(a_fin, q)] + [(b_send, q, k) for k in range(NCH)] + [(c_send, q)]
-    steps += [(b_core, 0, k) for k in range(NCH)] + [(b_core, 1, k) for k in range(NCH)]
+    steps = [(a_send, s) for s in range(WINDOW, min(12, WINDOW + 4))]
+    steps += [(a_fin, 0)] + [(b_send, 0, k) for k in range(NCH)] + [(c_send, 0)]
+    steps += [(a_send, s) for s in range(WINDOW + 4, 12)]
+    steps += [(a_fin, 1)] + [(b_send, 1, k) for k in range(NCH)] + [(c_send, 1)]
+    steps += [(a_fin, 2), (b_send, 2, 0), (b_send, 2, 1), (c_send, 2), (c_fwd, 0)]
+    steps += [(b_core, 0, k) for k in range(NCH)] + [(c_fwd, 1)]
+    steps += [(b_core, 1, k) for k in range(NCH)]
     steps += [
-        (b_core, 2, 0), (c_fwd, 0), (y_stage, 0), (d_send, 0),
-        (b_core, 2, 1), (y_stage, 1), (d_send, 1),
-        (c_fwd, 1), (b_core, 2, 2), (y_stage, 2), (d_send, 2),
-        (b_core, 2, 3), (y_stage, 3), (d_send, 3),
-        (c_fwd, 2), (d_fwd, 0), (d_fwd, 1), (c_fin, 0), (c_fin, 1), (c_fin, 2),
+        (b_core, 2, 0), (b_send, 2, 2), (y_stage, 0), (d_send, 0),
+        (b_core, 2, 1), (b_send, 2, 3), (c_fwd, 2), (y_stage, 1), (d_send, 1),
+        (b_core, 2, 2), (d_fwd, 0), (y_stage, 2), (d_send, 2),
+        (b_core, 2, 3), (d_fwd, 1), (y_stage, 3), (d_send, 3),
+        (c_fin, 0), (c_fin, 1), (c_fin, 2),
         (pair, 0), (pair, 1), (d_fwd, 2), (e2, 0), (e2, 1), (d_fwd, 3),
         (e3, 0), (pair, 2), (e3, 1), (pair, 3),
         (e4, 0), (e2, 2), (e4, 1), (e2, 3),

time: 125 us -> 114 us (0.912)
  Pallas kernels: 120 us -> 109 us
    pallas_call x1, Pallas kernels: 120 us -> 109 us  [local(): pl.pallas_call(kernel, name='exchange', out_shape=jax.ShapeDtypeStruct((B...]
where the time goes in v3:
time: 114 us; the launch traced here: 113 us
  Pallas kernels  109 us (96%)
  local copies, waits for them, and re-layouts  2.68 us (2%)
  other arithmetic  1.46 us (1%)
    pallas_call x1, Pallas kernels, local(): pl.pallas_call(kernel, name='exchange', out_shape=jax.ShapeDtypeStruct((B...  109 us

profile of v3, /device:TPU:1, one launch (start us, length us, event | category | flops | bytes accessed | tf_op | source)
XLA Modules:
  0.0 113.3 jit_solution(13210501582612314457)
XLA Ops:
  0.0 0.7 broadcast_multiply_fusion
  0.7 0.7 add.3
  1.5 0.6 reshape.8.index_ref
  2.1 109.1 %exchange.1 = bf16[256,1536]{1,0:T(8,128)(2,1)} custom-call(s32[16,256]{1,0:T(8,128)} %reshape.8.index_ref, s32[3,6]{1,0:T(4,128)} %cols_ref.1, s32[3]{0:T(128)} %counts_ref.1, bf16[1024,1536]{1,0:T(8,128)(2,1)} %orb_hbm.1, bf16[18,512,512]{2,1,0:T(8,128)(2,1)} %bitcast.3), custom_call_target="tpu_custom_call" | custom-call | flops 12000000000 | bytes 14000000 | tf_op jit(solution)/shard_map/exchange/pallas_call | solution.py:355
  111.2 2.1 %copy.8 = bf16[256,1536]{1,0:T(8,128)(2,1)} copy(bf16[256,1536]{1,0:T(8,128)(2,1)} %exchange.1) | data formatting | bytes 1572864

commit v4 on v3

--- a/solution.py
+++ b/solution.py
@@ -15,8 +15,9 @@
 COLS = 1536
 TILE = 512
 CAP = 32
-NSEM = 192
-WINDOW = 3
+NSEM = 200
+FORWARDED = 3
+WINDOW = 5
 
 
 def nt(a, b):
@@ -29,11 +30,11 @@
 
 def kernel(
     index_ref, cols_ref, counts_ref, orb_hbm, tiles_hbm, out_ref,
-    orb, tiles, onehot, slots_out, slots_in, xn, ev0, ev1, ev2, ev3, yg,
+    orb, tiles, onehot, slots_out, slots_in, xn, ev0, ev1, yg,
     pch, crecv, ysend, yrecv, sfull, rpart, fsend, frecv, ffwd, fsum, pos,
     ss, rs, ls,
 ):
-    every = (ev0, ev1, ev2, ev3)
+    every = (ev0, ev1)
     rows = BLK // NCH
     half = rows // 2
     g = lax.axis_index("grid")
@@ -102,39 +103,40 @@
 
     load_orb.wait()
     mine = pl.ds(pl.multiple_of(g * CAP, CAP), CAP)
-    pieces = [(q, dz) for q in range(3) for dz in (2, 1, 3, 0)]
+    groups = (
+        ((2, 1), (2, 3), (1, 2), (3, 2)),
+        ((2, 0), (0, 2), (2, 2)),
+        ((1, 1), (3, 3), (1, 3), (3, 1)),
+        ((1, 0), (3, 0), (0, 1), (0, 3)),
+    )
+    pieces = [(q, group) for q in range(3) for group in groups]
     a_copies = []
 
-    def a_rows(s):
-        q, dz = pieces[s]
-        part = pl.ds(pl.multiple_of(up(z, dz) * 128, 128), 128)
-        slots_out[q, part, :] = nn(
-            onehot[part, :], orb[:, q * TILE:(q + 1) * TILE]
-        ).astype(BF16)
+    def a_rows(q):
+        slots_out[q] = nn(onehot[...], orb[:, q * TILE:(q + 1) * TILE]).astype(BF16)
+        slots_in[q, mine, :] = slots_out[q, mine, :]
 
     def a_send(s):
         if s >= WINDOW:
             for copy in a_copies[s - WINDOW]:
                 copy.wait_send()
                 open_sends[:] = [other for other in open_sends if other is not copy]
-        q, dz = pieces[s]
-        group = []
-        for dx in (2, 1, 3, 0):
-            if (dz, dx) != (0, 0):
-                to = grid_of(z + dz, x + dx)
-                src = pl.ds(pl.multiple_of(to[0] * CAP, CAP), CAP)
-                group.append(send(slots_out.at[q, src], slots_in.at[q, mine], to))
-        a_copies.append(group)
-
-    for s in range(WINDOW):
-        a_rows(s)
-        if s == 0:
-            pl.semaphore_wait(bar, 19)
+        q, group = pieces[s]
+        sent = []
+        for dz, dx in group:
+            to = grid_of(z + dz, x + dx)
+            src = pl.ds(pl.multiple_of(to[0] * CAP, CAP), CAP)
+            sent.append(send(slots_out.at[q, src], slots_in.at[q, mine], to))
+        a_copies.append(sent)
+
+    a_rows(0)
+    pl.semaphore_wait(bar, 19)
+    for s in range(min(WINDOW, 4)):
         a_send(s)
-    for s in range(WINDOW, 12):
-        a_rows(s)
-    for q in range(3):
-        slots_in[q, mine, :] = slots_out[q, mine, :]
+    a_rows(1)
+    for s in range(4, WINDOW):
+        a_send(s)
+    a_rows(2)
 
     pos[0] = (index % 16).astype(F32)
     pos[1] = (index // 16 % 16).astype(F32)
@@ -157,35 +159,48 @@
         points = nn(unpermute, slots_in[q]).astype(BF16)
         xn[0, q, x] = points
         xn[1, q, z] = points
-        for k in range(NCH):
-            every[k][c * 12 + q * 4 + y] = points[k * rows:(k + 1) * rows, :]
-
-    def b_send(q, k):
-        src = every[k].at[c * 12 + q * 4 + y]
-        st["b", q, k] = [send(src, src, y_of(y + d)) for d in (2, 1, 3)]
-
-    def b_core(q, k):
-        for copy in st["b", q, k]:
+        for m in range(2):
+            every[m][c * 12 + q * 4 + y] = points[m * 128:(m + 1) * 128, :]
+
+    def b_send(q, m):
+        src = every[m].at[c * 12 + q * 4 + y]
+        ways = (1, 3) if q < FORWARDED else (2, 1, 3)
+        st["b", q, m] = [send(src, src, y_of(y + d)) for d in ways]
+
+    def b_fwd(q, m):
+        plus, minus = st["b", q, m]
+        plus.wait_recv()
+        src = every[m].at[c * 12 + q * 4 + up(y, -1), pl.ds(0, 64)]
+        forwarded = [send(src, src, y_of(y + 1))]
+        minus.wait_recv()
+        src = every[m].at[c * 12 + q * 4 + up(y, 1), pl.ds(64, 64)]
+        st["b", q, m] = forwarded + [send(src, src, y_of(y - 1))]
+
+    def b_core(q, m):
+        for copy in st["b", q, m]:
             copy.wait_recv()
-        src = every[k].at[pl.ds(c * 12 + q * 4, 4)]
-        st["bc", q, k] = send(src, src, core_peer)
-
-    def y_stage(k):
+        src = every[m].at[pl.ds(c * 12 + q * 4, 4)]
+        st["bc", q, m] = send(src, src, core_peer)
+
+    def y_stage(m):
         for q in range(3):
-            st["bc", q, k].wait_recv()
-        if k == 0:
+            st["bc", q, m].wait_recv()
+        if m == 0:
             load_tiles.wait()
         for r in range(3):
-            acc = jnp.zeros((rows, TILE), F32)
+            acc = jnp.zeros((128, TILE), F32)
             count = counts_ref[r]
             for s in range(6):
                 col = cols_ref[r, s]
-                block = every[k][(col // 3 % 2) * 12 + (col % 3) * 4 + col // 6]
+                block = every[m][(col // 3 % 2) * 12 + (col % 3) * 4 + col // 6]
                 if s > 0:
                     keep = (count > s).astype(F32)
                     block = block * keep.astype(BF16)
                 acc = acc + nt(block, tiles[r * 6 + s])
-            yg[place_of(k), k * rows:(k + 1) * rows, r * TILE:(r + 1) * TILE] = acc.astype(BF16)
+            acc = acc.astype(BF16)
+            cut = slice(r * TILE, (r + 1) * TILE)
+            yg[z, m * 128:m * 128 + 64, cut] = acc[:64]
+            yg[x, m * 128 + 64:m * 128 + 128, cut] = acc[64:]
 
     def place_of(k):
         return place[k % 2]
@@ -320,26 +335,26 @@
         out_ref[k * rows:k * rows + half, :] = lo.astype(BF16)
         out_ref[k * rows + half:(k + 1) * rows, :] = hi.astype(BF16)
 
+    both = range(2)
     steps = [(a_send, s) for s in range(WINDOW, min(12, WINDOW + 4))]
-    steps += [(a_fin, 0)] + [(b_send, 0, k) for k in range(NCH)] + [(c_send, 0)]
+    steps += [(a_fin, 0)] + [(b_send, 0, m) for m in both] + [(c_send, 0)]
     steps += [(a_send, s) for s in range(WINDOW + 4, 12)]
-    steps += [(a_fin, 1)] + [(b_send, 1, k) for k in range(NCH)] + [(c_send, 1)]
-    steps += [(a_fin, 2), (b_send, 2, 0), (b_send, 2, 1), (c_send, 2), (c_fwd, 0)]
-    steps += [(b_core, 0, k) for k in range(NCH)] + [(c_fwd, 1)]
-    steps += [(b_core, 1, k) for k in range(NCH)]
+    steps += [(a_fin, 1)] + [(b_send, 1, m) for m in both]
+    steps += [(b_fwd, 0, m) for m in both] + [(c_send, 1)]
+    steps += [(a_fin, 2), (b_send, 2, 0)] + [(b_fwd, 1, m) for m in both]
+    steps += [(b_send, 2, 1), (c_send, 2)]
+    steps += [(b_core, q, m) for q in both for m in both]
     steps += [
-        (b_core, 2, 0), (b_send, 2, 2), (y_stage, 0), (d_send, 0),
-        (b_core, 2, 1), (b_send, 2, 3), (c_fwd, 2), (y_stage, 1), (d_send, 1),
-        (b_core, 2, 2), (d_fwd, 0), (y_stage, 2), (d_send, 2),
-        (b_core, 2, 3), (d_fwd, 1), (y_stage, 3), (d_send, 3),
+        (b_fwd, 2, 0), (c_fwd, 0), (b_fwd, 2, 1), (b_core, 2, 0), (c_fwd, 1),
+        (y_stage, 0), (d_send, 0), (d_send, 1), (c_fwd, 2),
+        (b_core, 2, 1), (y_stage, 1), (d_fwd, 0), (d_fwd, 1), (d_send, 2), (d_send, 3),
         (c_fin, 0), (c_fin, 1), (c_fin, 2),
-        (pair, 0), (pair, 1), (d_fwd, 2), (e2, 0), (e2, 1), (d_fwd, 3),
-        (e3, 0), (pair, 2), (e3, 1), (pair, 3),
-        (e4, 0), (e2, 2), (e4, 1), (e2, 3),
-        (res, 0), (e3, 2), (res, 1), (e3, 3), (e4, 2), (e4, 3),
-        (f_fwd, 0), (f_fwd, 1), (res, 2), (res, 3), (f_fwd, 2), (f_fwd, 3),
+        (pair, 0), (pair, 1), (e2, 0), (e2, 1), (d_fwd, 2), (d_fwd, 3),
+        (e3, 0), (e3, 1), (pair, 2), (pair, 3), (e2, 2), (e4, 0), (e2, 3), (e4, 1),
+        (res, 0), (res, 1), (e3, 2), (e3, 3), (f_fwd, 0), (f_fwd, 1),
+        (e4, 2), (e4, 3), (res, 2), (res, 3), (f_fin, 0), (f_fin, 1), (f_fwd, 2), (f_fwd, 3),
     ]
-    steps += [(f_fin, k) for k in range(NCH)]
+    steps += [(f_fin, 2), (f_fin, 3)]
     for stage, *at in steps:
         stage(*at)
     for copy in open_sends:
@@ -365,10 +380,8 @@
             pltpu.VMEM((3, 512, TILE), BF16),
             pltpu.VMEM((3, 512, TILE), BF16),
             pltpu.VMEM((2, 3, 4, BLK, TILE), BF16),
-            pltpu.VMEM((24, rows, TILE), BF16),
-            pltpu.VMEM((24, rows, TILE), BF16),
-            pltpu.VMEM((24, rows, TILE), BF16),
-            pltpu.VMEM((24, rows, TILE), BF16),
+            pltpu.VMEM((24, 128, TILE), BF16),
+            pltpu.VMEM((24, 128, TILE), BF16),
             pltpu.VMEM((4, BLK, COLS), BF16),
             pltpu.VMEM((NCH, 2, 4 * rows, TILE), F32),
             pltpu.VMEM((NCH, 4 * rows, TILE), F32),

time: 114 us -> 110 us (0.965)
  Pallas kernels: 109 us -> 105 us
    pallas_call x1, Pallas kernels: 109 us -> 105 us  [local(): pl.pallas_call(kernel, name='exchange', out_shape=jax.ShapeDtypeStruct((B...]
where the time goes in v4:
time: 110 us
  Pallas kernels  105 us (95%)
  local copies, waits for them, and re-layouts  2.68 us (2%)
  other arithmetic  1.46 us (1%)
    pallas_call x1, Pallas kernels, local(): pl.pallas_call(kernel, name='exchange', out_shape=jax.ShapeDtypeStruct((B...  105 us

profile of v4, /device:TPU:1, one launch (start us, length us, event | category | flops | bytes accessed | tf_op | source)
XLA Modules:
  0.0 109.6 jit_solution(15630120474620331737)
XLA Ops:
  0.0 0.7 broadcast_multiply_fusion
  0.7 0.7 add.3
  1.5 0.6 reshape.8.index_ref
  2.1 105.5 %exchange.1 = bf16[256,1536]{1,0:T(8,128)(2,1)} custom-call(s32[16,256]{1,0:T(8,128)} %reshape.8.index_ref, s32[3,6]{1,0:T(4,128)} %cols_ref.1, s32[3]{0:T(128)} %counts_ref.1, bf16[1024,1536]{1,0:T(8,128)(2,1)} %orb_hbm.1, bf16[18,512,512]{2,1,0:T(8,128)(2,1)} %bitcast.3), custom_call_target="tpu_custom_call" | custom-call | flops 12000000000 | bytes 14000000 | tf_op jit(solution)/shard_map/exchange/pallas_call | solution.py:370
  107.5 2.1 %copy.8 = bf16[256,1536]{1,0:T(8,128)(2,1)} copy(bf16[256,1536]{1,0:T(8,128)(2,1)} %exchange.1) | data formatting | bytes 1572864

commit v5 on v4

--- a/solution.py
+++ b/solution.py
@@ -70,6 +70,9 @@
         open_sends.append(copy)
         return copy
 
+    load_orb = pltpu.make_async_copy(orb_hbm, orb, ls.at[0])
+    load_orb.start()
+
     bar = pltpu.get_barrier_semaphore()
     for dz in (2, 1, 3, 0):
         for dx in (2, 1, 3, 0):
@@ -81,10 +84,6 @@
         pl.semaphore_signal(bar, inc=1, device_id=y_of(y + dy), device_id_type=MESH)
     pl.semaphore_signal(bar, inc=1, device_id=core_peer, device_id_type=MESH)
 
-    load_orb = pltpu.make_async_copy(orb_hbm, orb, ls.at[0])
-    load_orb.start()
-    load_tiles = pltpu.make_async_copy(tiles_hbm, tiles, ls.at[1])
-    load_tiles.start()
 
     index = index_ref[...]
     owner = index // 1024
@@ -102,6 +101,8 @@
         onehot[i * CAP:(i + 1) * CAP, :] = (grid_row == wanted).astype(F32).astype(BF16)
 
     load_orb.wait()
+    load_tiles = pltpu.make_async_copy(tiles_hbm, tiles, ls.at[1])
+    load_tiles.start()
     mine = pl.ds(pl.multiple_of(g * CAP, CAP), CAP)
     groups = (
         ((2, 1), (2, 3), (1, 2), (3, 2)),
@@ -350,7 +351,7 @@
         (b_core, 2, 1), (y_stage, 1), (d_fwd, 0), (d_fwd, 1), (d_send, 2), (d_send, 3),
         (c_fin, 0), (c_fin, 1), (c_fin, 2),
         (pair, 0), (pair, 1), (e2, 0), (e2, 1), (d_fwd, 2), (d_fwd, 3),
-        (e3, 0), (e3, 1), (pair, 2), (pair, 3), (e2, 2), (e4, 0), (e2, 3), (e4, 1),
+        (e3, 0), (e3, 1), (pair, 2), (pair, 3), (e2, 2), (e2, 3), (e4, 0), (e4, 1),
         (res, 0), (res, 1), (e3, 2), (e3, 3), (f_fwd, 0), (f_fwd, 1),
         (e4, 2), (e4, 3), (res, 2), (res, 3), (f_fin, 0), (f_fin, 1), (f_fwd, 2), (f_fwd, 3),
     ]

time: 110 us -> 110 us (level)
  no operation moved by 1% of the time
where the time goes in v5:
time: 110 us
  Pallas kernels  105 us (95%)
  local copies, waits for them, and re-layouts  2.68 us (2%)
  other arithmetic  1.46 us (1%)
    pallas_call x1, Pallas kernels, local(): pl.pallas_call(kernel, name='exchange', out_shape=jax.ShapeDtypeStruct((B...  105 us

profile of v5, /device:TPU:1, one launch (start us, length us, event | category | flops | bytes accessed | tf_op | source)
XLA Modules:
  0.0 109.6 jit_solution(14307618735133198694)
XLA Ops:
  0.0 0.7 broadcast_multiply_fusion
  0.7 0.7 add.3
  1.5 0.6 reshape.8.index_ref
  2.1 105.5 %exchange.1 = bf16[256,1536]{1,0:T(8,128)(2,1)} custom-call(s32[16,256]{1,0:T(8,128)} %reshape.8.index_ref, s32[3,6]{1,0:T(4,128)} %cols_ref.1, s32[3]{0:T(128)} %counts_ref.1, bf16[1024,1536]{1,0:T(8,128)(2,1)} %orb_hbm.1, bf16[18,512,512]{2,1,0:T(8,128)(2,1)} %bitcast.3), custom_call_target="tpu_custom_call" | custom-call | flops 12000000000 | bytes 14000000 | tf_op jit(solution)/shard_map/exchange/pallas_call | solution.py:371
  107.5 2.1 %copy.8 = bf16[256,1536]{1,0:T(8,128)(2,1)} copy(bf16[256,1536]{1,0:T(8,128)(2,1)} %exchange.1) | data formatting | bytes 1572864

commit v6 on v4

--- a/solution.py
+++ b/solution.py
@@ -31,7 +31,7 @@
 def kernel(
     index_ref, cols_ref, counts_ref, orb_hbm, tiles_hbm, out_ref,
     orb, tiles, onehot, slots_out, slots_in, xn, ev0, ev1, yg,
-    pch, crecv, ysend, yrecv, sfull, rpart, fsend, frecv, ffwd, fsum, pos,
+    pch, csend, crecv, ysend, yrecv, sfull, rpart, fsend, frecv, ffwd, fsum, pos,
     ss, rs, ls,
 ):
     every = (ev0, ev1)
@@ -251,14 +251,16 @@
                 rhs = xn[mode, q, pl.ds(2 * h, 2)]
                 term = nt(lhs.reshape(4 * rows, TILE), rhs.reshape(2 * BLK, TILE))
                 total = term if total is None else total + term
-            pch[k, h] = total
             if h is o:
-                st["e1", k] = send(pch.at[k, o], crecv.at[k], core_peer)
+                csend[k] = total.astype(BF16)
+                st["e1", k] = send(csend.at[k], crecv.at[k], core_peer)
+            else:
+                pch[k] = total
 
     def e2(k):
         st["e1", k].wait_recv()
-        total = pch[k, c] + crecv[k]
-        pch[k, c] = total
+        total = pch[k] + crecv[k].astype(F32)
+        pch[k] = total
         ysend[k] = total.astype(BF16).reshape(4, rows, TILE)
         for d in (2, 1, 3):
             st["e2", k, d] = send(
@@ -267,7 +269,7 @@
 
     def e3(k):
         part = pl.ds(pl.multiple_of(y * rows, rows), rows)
-        total = pch[k, c, part, :]
+        total = pch[k, part, :]
         for d in (1, 2, 3):
             st["e2", k, d].wait_recv()
             total = total + yrecv[k, d - 1].astype(F32)
@@ -337,11 +339,11 @@
 
     both = range(2)
     steps = [(a_send, s) for s in range(WINDOW, min(12, WINDOW + 4))]
-    steps += [(a_fin, 0)] + [(b_send, 0, m) for m in both] + [(c_send, 0)]
+    steps += [(a_fin, 0)] + [(b_send, 0, m) for m in both]
     steps += [(a_send, s) for s in range(WINDOW + 4, 12)]
     steps += [(a_fin, 1)] + [(b_send, 1, m) for m in both]
-    steps += [(b_fwd, 0, m) for m in both] + [(c_send, 1)]
-    steps += [(a_fin, 2), (b_send, 2, 0)] + [(b_fwd, 1, m) for m in both]
+    steps += [(b_fwd, 0, m) for m in both]
+    steps += [(a_fin, 2), (b_send, 2, 0), (c_send, 0), (c_send, 1)] + [(b_fwd, 1, m) for m in both]
     steps += [(b_send, 2, 1), (c_send, 2)]
     steps += [(b_core, q, m) for q in both for m in both]
     steps += [
@@ -383,8 +385,9 @@
             pltpu.VMEM((24, 128, TILE), BF16),
             pltpu.VMEM((24, 128, TILE), BF16),
             pltpu.VMEM((4, BLK, COLS), BF16),
-            pltpu.VMEM((NCH, 2, 4 * rows, TILE), F32),
             pltpu.VMEM((NCH, 4 * rows, TILE), F32),
+            pltpu.VMEM((NCH, 4 * rows, TILE), BF16),
+            pltpu.VMEM((NCH, 4 * rows, TILE), BF16),
             pltpu.VMEM((NCH, 4, rows, TILE), BF16),
             pltpu.VMEM((NCH, 3, rows, TILE), BF16),
             pltpu.VMEM((NCH, 2, 4, rows, TILE), BF16),

time: 110 us -> 110 us (level)
  no operation moved by 1% of the time
where the time goes in v6:
time: 110 us; the launch traced here: 109 us
  Pallas kernels  105 us (95%)
  local copies, waits for them, and re-layouts  2.68 us (2%)
  other arithmetic  1.46 us (1%)
    pallas_call x1, Pallas kernels, local(): pl.pallas_call(kernel, name='exchange', out_shape=jax.ShapeDtypeStruct((B...  105 us

profile of v6, /device:TPU:1, one launch (start us, length us, event | category | flops | bytes accessed | tf_op | source)
XLA Modules:
  0.0 109.3 jit_solution(3339758620358408841)
XLA Ops:
  0.0 0.7 broadcast_multiply_fusion
  0.7 0.7 add.3
  1.5 0.6 reshape.8.index_ref
  2.1 105.1 %exchange.1 = bf16[256,1536]{1,0:T(8,128)(2,1)} custom-call(s32[16,256]{1,0:T(8,128)} %reshape.8.index_ref, s32[3,6]{1,0:T(4,128)} %cols_ref.1, s32[3]{0:T(128)} %counts_ref.1, bf16[1024,1536]{1,0:T(8,128)(2,1)} %orb_hbm.1, bf16[18,512,512]{2,1,0:T(8,128)(2,1)} %bitcast.3), custom_call_target="tpu_custom_call" | custom-call | flops 12000000000 | bytes 14000000 | tf_op jit(solution)/shard_map/exchange/pallas_call | solution.py:372
  107.2 2.1 %copy.8 = bf16[256,1536]{1,0:T(8,128)(2,1)} copy(bf16[256,1536]{1,0:T(8,128)(2,1)} %exchange.1) | data formatting | bytes 1572864
